TPU v7x, 32 devices: a whole 2x2x4 slice. The times are simulated.
32 devices in a mesh: grp: 2 (over x), ka: 16 (over z, y, core).
Axes of the slice: x: 2, y: 2, z: 4, core: 2. Of those that a mesh axis runs over, the one named last changes fastest.
Arguments:
- wannier_table: float32 [2, 2048, 8192], P(None, 'grp', 'ka'), parts along dimension 1, may hold values from -0.125 to 0.125
- lattice: int32 [3, 2048], P(None, 'grp'), parts along dimension 1, may hold values from -12 to 12
- kpoint_grid: int32 [3, 2048], P(None, ('grp', 'ka')), parts along dimension 1, may hold values from 0 to 63
- eigen_vectors: float32 [2048, 64, 128], P(('grp', 'ka')), parts along dimension 0, may hold values from -0.5 to 0.5
- target_owner: int32 [2048], P(('grp', 'ka')), parts along dimension 0, may hold values from 0 to 15, as said below
- target_slot: int32 [2048], P(('grp', 'ka')), parts along dimension 0, may hold values from 0 to 63
Outputs:
- rotated_coupling: float32 [2048, 2, 64, 128], P(('grp', 'ka')), parts along dimension 0
There are 2 independent parts, one for each index of `grp`. A program takes and returns all parts, laid end to end along the dimension named above; each array names one. Nothing has to cross between parts.
Inputs may be any that keep to these rules, and one draw needn't show every extreme that they name: target_owner[k] * 64 + target_slot[k] over all k is a permutation of the 1024 k-points. The 64 k-points of one index of ka ask at most 8 of them of any one owner, and every device asks exactly 8 of some owner.
All inputs are finite; a program needn't handle non-finite values.
Results may differ from a plain program's by a relative error of at most 0.0003.
Values sent between devices are 32-bit elements; how exact they have to be, the bound alone decides.
A program may use at most 128 MiB of HBM per device.

v0:
```python
import functools
import math

import jax
import jax.numpy as jnp
from jax import lax
from jax.experimental import pallas as pl
from jax.experimental.pallas import tpu as pltpu
from jax.sharding import PartitionSpec as P

KMESH = 64
MESH = pl.DeviceIdType.MESH


def phase_matrix(grid_block, lattice):
    products = (
        grid_block[0][:, None] * lattice[0][None, :]
        + grid_block[1][:, None] * lattice[1][None, :]
        + grid_block[2][:, None] * lattice[2][None, :]
    )
    angles = jnp.mod(products, KMESH).astype(jnp.float32) * (2.0 * math.pi / KMESH)
    cosine = jnp.cos(angles)
    sine_part = jnp.sin(angles)
    upper_rows = jnp.concatenate([cosine, -sine_part], 1)
    lower_rows = jnp.concatenate([sine_part, cosine], 1)
    return jnp.concatenate([upper_rows, lower_rows], 0)


def rotate(real_part, imag_part, near_vectors, far_vectors):
    orbitals = near_vectors.shape[1]
    highest = lax.Precision.HIGHEST
    near_swap = jnp.concatenate([-near_vectors[..., orbitals:], near_vectors[..., :orbitals]], -1)
    right_done = jnp.einsum(
        "kamn,knj->kamj", real_part, near_vectors, precision=highest
    ) + jnp.einsum("kamn,knj->kamj", imag_part, near_swap, precision=highest)
    right_swap = jnp.concatenate([right_done[..., orbitals:], -right_done[..., :orbitals]], -1)
    return jnp.einsum(
        "kmi,kamj->kaij", far_vectors[..., :orbitals], right_done, precision=highest
    ) + jnp.einsum("kmi,kamj->kaij", far_vectors[..., orbitals:], right_swap, precision=highest)


def fetch_far(eigen_vectors, target_owner, target_slot, devices):
    kpoints = eigen_vectors.shape[0]
    orbitals = eigen_vectors.shape[1]
    capacity = 2 * kpoints // devices
    owners_onehot = (target_owner[:, None] == jnp.arange(devices, dtype=jnp.int32)[None, :]).astype(
        jnp.int32
    )
    before = jnp.cumsum(owners_onehot, 0) - owners_onehot
    position = jnp.sum(before * owners_onehot, 1)
    flat_index = target_owner * capacity + position
    wanted = (
        jnp.zeros((devices * capacity,), jnp.int32)
        .at[flat_index]
        .set(target_slot)
        .reshape(devices, capacity)
    )
    picked = eigen_vectors[lax.all_to_all(wanted, "ka", split_axis=0, concat_axis=0, tiled=True)]
    fetched = lax.all_to_all(picked, "ka", split_axis=0, concat_axis=0, tiled=True)
    return fetched.reshape(devices * capacity, orbitals, 2 * orbitals)[flat_index]


def interpolate(wannier_table, lattice, kpoint_grid, kpoints, devices):
    vectors = wannier_table.shape[1]
    local_pairs = wannier_table.shape[2]
    highest = lax.Precision.HIGHEST
    grid_all = lax.all_gather(kpoint_grid, "ka", axis=1, tiled=True)
    per_block = 1
    while (
        per_block * 2 <= devices
        and devices % (per_block * 2) == 0
        and (per_block * 2 * kpoints <= 512)
    ):
        per_block = per_block * 2
    block_rows = per_block * kpoints
    flat_table = wannier_table.reshape(2 * vectors, local_pairs)

    def fill_block(block_id, collected):
        grid_block = lax.dynamic_slice_in_dim(grid_all, block_id * block_rows, block_rows, 1)
        result = jnp.dot(
            phase_matrix(grid_block, lattice),
            flat_table,
            precision=highest,
            preferred_element_type=jnp.float32,
        )
        return lax.dynamic_update_slice_in_dim(
            collected, result.reshape(2, block_rows, local_pairs), block_id * block_rows, 1
        )

    initial = jnp.zeros((2, kpoints * devices, local_pairs), jnp.float32)
    computed = lax.fori_loop(0, devices // per_block, fill_block, initial)
    return lax.all_to_all(computed, "ka", split_axis=1, concat_axis=2, tiled=True)


def local(wannier_table, lattice, kpoint_grid, eigen_vectors, target_owner, target_slot):
    kpoints = eigen_vectors.shape[0]
    orbitals = eigen_vectors.shape[1]
    devices = lax.axis_size("ka")
    interpolated = interpolate(wannier_table, lattice, kpoint_grid, kpoints, devices)
    far_vectors = fetch_far(eigen_vectors, target_owner, target_slot, devices)
    real_part = interpolated[0].reshape(kpoints, -1, orbitals, orbitals)
    imag_part = interpolated[1].reshape(kpoints, -1, orbitals, orbitals)
    return rotate(real_part, imag_part, eigen_vectors, far_vectors)


def cos_sin(index):
    quarter = KMESH // 4
    shifted = index + quarter // 2
    quadrant = shifted // quarter if quarter & (quarter - 1) else shifted >> (quarter.bit_length() - 1)
    arc = (index - quadrant * quarter).astype(jnp.float32) * (2.0 * math.pi / KMESH)
    square = arc * arc
    sine = arc * (
        1.0 + square * (-1.0 / 6 + square * (1.0 / 120 + square * (-1.0 / 5040 + square * (1.0 / 362880))))
    )
    cosine = 1.0 + square * (
        -0.5
        + square
        * (1.0 / 24 + square * (-1.0 / 720 + square * (1.0 / 40320 + square * (-1.0 / 3628800))))
    )
    swapped = (quadrant & 1) == 1
    out_cos = jnp.where(swapped, sine, cosine)
    out_sin = jnp.where(swapped, cosine, sine)
    out_cos = jnp.where(((quadrant + 1) & 2) == 2, -out_cos, out_cos)
    out_sin = jnp.where((quadrant & 2) == 2, -out_sin, out_sin)
    return out_cos, out_sin


def split(value):
    high = value.astype(jnp.bfloat16)
    return high, (value - high.astype(jnp.float32)).astype(jnp.bfloat16)


def dot(left, right):
    return jnp.dot(left, right, preferred_element_type=jnp.float32)


def kernel(
    sizes,
    table_hbm,
    eigen_hbm,
    letters,
    lattice,
    flat_index,
    out_hbm,
    table,
    eigen,
    table_high,
    table_low,
    inbox,
    inbox_scalar,
    far_out,
    far_in,
    entries_out,
    entries_in,
    waves,
    near_parts,
    far_parts,
    result,
    load_sem,
    scalar_sem,
    letter_send,
    letter_recv,
    far_send,
    far_recv,
    entry_send,
    entry_recv,
    store_sem,
):
    n, kpoints, orbitals, vectors, pairs, capacity, per_group, chunks = sizes
    rows = pairs // orbitals
    wide = 2 * orbitals
    modes = n * rows // orbitals
    per_chunk = kpoints // chunks
    me = lax.axis_index("ka")

    load_table = pltpu.make_async_copy(table_hbm, table, load_sem.at[0])
    load_eigen = pltpu.make_async_copy(eigen_hbm, eigen, load_sem.at[1])
    load_eigen.start()
    load_table.start()

    barrier = pltpu.get_barrier_semaphore()

    @pl.loop(1, n)
    def _(step):
        other = lax.rem(me + step, n)
        pl.semaphore_signal(barrier, inc=1, device_id={"ka": other}, device_id_type=MESH)

    pl.semaphore_wait(barrier, n - 1)

    def send_letter(step):
        other = lax.rem(me + step, n)
        return pltpu.make_async_remote_copy(
            src_ref=letters.at[other],
            dst_ref=inbox.at[me],
            send_sem=letter_send.at[other],
            recv_sem=letter_recv.at[me],
            device_id={"ka": other},
            device_id_type=MESH,
        )

    def recv_letter(step):
        other = lax.rem(me + step, n)
        return pltpu.make_async_remote_copy(
            src_ref=letters.at[other],
            dst_ref=inbox.at[other],
            send_sem=letter_send.at[other],
            recv_sem=letter_recv.at[other],
            device_id={"ka": other},
            device_id_type=MESH,
        )

    def send_far(step):
        other = lax.rem(me + step, n)
        return pltpu.make_async_remote_copy(
            src_ref=far_out.at[other],
            dst_ref=far_in.at[me],
            send_sem=far_send.at[other],
            recv_sem=far_recv.at[me],
            device_id={"ka": other},
            device_id_type=MESH,
        )

    def recv_far(step):
        other = lax.rem(me + step, n)
        return pltpu.make_async_remote_copy(
            src_ref=far_out.at[other],
            dst_ref=far_in.at[other],
            send_sem=far_send.at[other],
            recv_sem=far_recv.at[other],
            device_id={"ka": other},
            device_id_type=MESH,
        )

    def entries(step, chunk, receive):
        other = lax.rem(me + step, n)
        part = pl.ds(chunk * per_chunk * rows, per_chunk * rows)
        slot = other if receive else me
        return pltpu.make_async_remote_copy(
            src_ref=entries_out.at[other, part],
            dst_ref=entries_in.at[slot, part],
            send_sem=entry_send.at[other, chunk],
            recv_sem=entry_recv.at[slot, chunk],
            device_id={"ka": other},
            device_id_type=MESH,
        )

    @pl.loop(1, n)
    def _(step):
        send_letter(step).start()

    inbox[me] = letters[me]

    @pl.loop(1, n)
    def _(step):
        recv_letter(step).wait_recv()

    to_scalar = pltpu.make_async_copy(inbox, inbox_scalar, scalar_sem.at[0])
    to_scalar.start()
    to_scalar.wait()
    load_eigen.wait()

    def far_order(step):
        return lax.rem(step + n // 2, n)

    @pl.loop(0, n)
    def _(step):
        offset = far_order(step)
        other = lax.rem(me + offset, n)
        for slot in range(capacity):
            far_out[other, slot] = eigen[inbox_scalar[other, 3, slot]]

        @pl.when(offset != 0)
        def _():
            send_far(offset).start()

    own_far = pltpu.make_async_copy(far_out.at[me], far_in.at[me], scalar_sem.at[1])
    own_far.start()

    load_table.wait()
    piece = 128

    @pl.loop(0, vectors // piece)
    def _(step):
        part = pl.ds(pl.multiple_of(step * piece, piece), piece)
        for which in range(2):
            high, low = split(table[which, part, :])
            table_high[which, part, :] = high
            table_low[which, part, :] = low

    group_rows = per_group * kpoints
    lanes = lax.broadcasted_iota(jnp.int32, (group_rows, wide), 1)
    first_half = lanes < orbitals

    @pl.loop(0, n // per_group)
    def _(group):
        for local_at in range(per_group):
            other = lax.rem(me + far_order(group * per_group + local_at), n)
            turned = inbox[other].T
            coords = [turned[:kpoints, axis : axis + 1] for axis in range(3)]

            @pl.loop(0, vectors // piece)
            def _(step):
                part = pl.ds(pl.multiple_of(step * piece, piece), piece)
                products = (
                    coords[0] * lattice[0:1, part]
                    + coords[1] * lattice[1:2, part]
                    + coords[2] * lattice[2:3, part]
                )
                cosine, sine = cos_sin(products & (KMESH - 1))
                own_rows = pl.ds(local_at * kpoints, kpoints)
                cos_high, cos_low = split(cosine)
                sin_high, sin_low = split(sine)
                waves[0, own_rows, part] = cos_high
                waves[1, own_rows, part] = cos_low
                waves[2, own_rows, part] = sin_high
                waves[3, own_rows, part] = sin_low

        block = min(256, pairs)
        for first in range(0, pairs, block):
            cols = slice(first, first + block)

            def product(wave, which):
                return (
                    dot(waves[wave], table_high[which, :, cols])
                    + dot(waves[wave], table_low[which, :, cols])
                    + dot(waves[wave + 1], table_high[which, :, cols])
                )

            real = product(0, 0) - product(2, 1)
            imag = product(0, 1) + product(2, 0)
            for pair in range(block // wide):
                span = slice(pair * wide, (pair + 1) * wide)
                real_part, imag_part = real[:, span], imag[:, span]
                even = jnp.where(first_half, real_part, pltpu.roll(imag_part, orbitals, 1))
                odd = jnp.where(first_half, pltpu.roll(real_part, orbitals, 1), imag_part)
                row = first // orbitals + 2 * pair
                for local_at in range(per_group):
                    other = lax.rem(me + far_order(group * per_group + local_at), n)
                    own = slice(local_at * kpoints, (local_at + 1) * kpoints)
                    entries_out[other, pl.ds(row, kpoints, stride=rows), :] = even[own]
                    entries_out[other, pl.ds(row + 1, kpoints, stride=rows), :] = odd[own]

    for chunk in range(chunks):

        @pl.loop(0, n)
        def _(step):
            offset = far_order(step)

            @pl.when(offset != 0)
            def _():
                entries(offset, chunk, False).start()

    own_entries = pltpu.make_async_copy(entries_out.at[me], entries_in.at[me], scalar_sem.at[2])
    own_entries.start()

    half_lane = lax.broadcasted_iota(jnp.int32, (orbitals, wide), 1) < orbitals

    @pl.loop(0, kpoints)
    def _(k):
        near = eigen[k]
        turned = pltpu.roll(near, orbitals, 1)
        lower = jnp.where(half_lane, -turned, turned)
        high, low = split(jnp.concatenate([near, lower], 0))
        near_parts[k] = jnp.concatenate([high, low], 1)

    own_far.wait()

    @pl.loop(1, n)
    def _(step):
        recv_far(step).wait_recv()

    @pl.loop(0, kpoints)
    def _(k):
        at = flat_index[k]
        far = far_in[at // capacity, lax.rem(at, capacity)]
        high = far.astype(jnp.bfloat16).astype(jnp.float32)
        far_parts[k] = jnp.concatenate([high, far - high], 0).T.astype(jnp.bfloat16)

    own_entries.wait()

    def rotate_one(k):
        matrix = entries_in[:, pl.ds(pl.multiple_of(k * rows, rows), rows), :].reshape(n * rows, wide)
        high, low = split(matrix)
        near = near_parts[k]
        right = dot(jnp.concatenate([high, low], 1), jnp.concatenate([near, near], 0))
        right = right[:, :wide] + right[:, wide:]
        right = jnp.concatenate(
            [right[mode * orbitals : (mode + 1) * orbitals] for mode in range(modes)], 1
        )
        high, low = split(right)
        far = far_parts[k]
        both = dot(jnp.concatenate([far, far], 1), jnp.concatenate([high, high, low, low], 0))
        for mode in range(modes):
            span = both[:, mode * wide : (mode + 1) * wide]
            turned = pltpu.roll(span[orbitals:], orbitals, 1)
            result[k, mode] = span[:orbitals] + jnp.where(half_lane, turned, -turned)

    def store(chunk):
        part = pl.ds(chunk * per_chunk, per_chunk)
        return pltpu.make_async_copy(result.at[part], out_hbm.at[part], store_sem.at[chunk])

    together = 2 if per_chunk % 2 == 0 else 1
    for chunk in range(chunks):

        @pl.loop(1, n)
        def _(step):
            entries(step, chunk, True).wait_recv()

        @pl.loop(0, per_chunk // together)
        def _(step):
            for extra in range(together):
                rotate_one(chunk * per_chunk + step * together + extra)

        store(chunk).start()

    for chunk in range(chunks):
        store(chunk).wait()

        @pl.loop(1, n)
        def _(step):
            entries(step, chunk, False).wait_send()

    @pl.loop(1, n)
    def _(step):
        send_letter(step).wait_send()
        send_far(step).wait_send()


def fused(wannier_table, lattice, kpoint_grid, eigen_vectors, target_owner, target_slot):
    n = lax.axis_size("ka")
    kpoints, orbitals, wide = eigen_vectors.shape
    vectors, pairs = wannier_table.shape[1:]
    capacity = 2 * kpoints // n
    rows = pairs // orbitals
    modes = n * rows // orbitals
    per_group = math.gcd(n, 4)
    chunks = math.gcd(kpoints, 4)

    ids = jnp.arange(kpoints, dtype=jnp.int32)
    same = (target_owner[:, None] == target_owner[None, :]) & (ids[None, :] < ids[:, None])
    position = jnp.sum(same.astype(jnp.int32), 1)
    flat_index = target_owner * capacity + position
    places = jnp.arange(n * capacity, dtype=jnp.int32)
    wanted = jnp.sum(
        jnp.where(places[:, None] == flat_index[None, :], target_slot[None, :], 0), 1
    ).reshape(n, 1, capacity)
    wanted = jnp.pad(wanted, ((0, 0), (3, 4), (0, 128 - capacity)))
    letters = wanted + jnp.pad(kpoint_grid, ((0, 5), (0, 128 - kpoints)))[None]

    f32, bf16 = jnp.float32, jnp.bfloat16
    sizes = (n, kpoints, orbitals, vectors, pairs, capacity, per_group, chunks)
    return pl.pallas_call(
        functools.partial(kernel, sizes),
        out_shape=jax.ShapeDtypeStruct((kpoints, modes, orbitals, wide), f32),
        in_specs=[
            pl.BlockSpec(memory_space=pl.ANY),
            pl.BlockSpec(memory_space=pl.ANY),
            pl.BlockSpec(memory_space=pltpu.VMEM),
            pl.BlockSpec(memory_space=pltpu.VMEM),
            pl.BlockSpec(memory_space=pltpu.SMEM),
        ],
        out_specs=pl.BlockSpec(memory_space=pl.ANY),
        scratch_shapes=[
            pltpu.VMEM((2, vectors, pairs), f32),
            pltpu.VMEM((kpoints, orbitals, wide), f32),
            pltpu.VMEM((2, vectors, pairs), bf16),
            pltpu.VMEM((2, vectors, pairs), bf16),
            pltpu.VMEM((n, 8, 128), jnp.int32),
            pltpu.SMEM((n, 8, 128), jnp.int32),
            pltpu.VMEM((n, capacity, orbitals, wide), f32),
            pltpu.VMEM((n, capacity, orbitals, wide), f32),
            pltpu.VMEM((n, kpoints * rows, wide), f32),
            pltpu.VMEM((n, kpoints * rows, wide), f32),
            pltpu.VMEM((4, per_group * kpoints, vectors), bf16),
            pltpu.VMEM((kpoints, wide, 2 * wide), bf16),
            pltpu.VMEM((kpoints, wide, wide), bf16),
            pltpu.VMEM((kpoints, modes, orbitals, wide), f32),
            pltpu.SemaphoreType.DMA((2,)),
            pltpu.SemaphoreType.DMA((3,)),
            pltpu.SemaphoreType.DMA((n,)),
            pltpu.SemaphoreType.DMA((n,)),
            pltpu.SemaphoreType.DMA((n,)),
            pltpu.SemaphoreType.DMA((n,)),
            pltpu.SemaphoreType.DMA((n, chunks)),
            pltpu.SemaphoreType.DMA((n, chunks)),
            pltpu.SemaphoreType.DMA((chunks,)),
        ],
        compiler_params=pltpu.CompilerParams(
            collective_id=0, has_side_effects=True, vmem_limit_bytes=60 * 1024 * 1024
        ),
    )(wannier_table, eigen_vectors, letters, lattice, flat_index)


def part(wannier_table, lattice, kpoint_grid, eigen_vectors, target_owner, target_slot):
    rows = wannier_table.shape[2] // eigen_vectors.shape[1]
    tiled = rows % 8 == 0 and wannier_table.shape[1] % 128 == 0 and eigen_vectors.shape[2] == 128
    step = fused if tiled else local
    return step(wannier_table, lattice, kpoint_grid, eigen_vectors, target_owner, target_slot)


def solution(mesh):
    placed = (
        P(None, "grp", "ka"),
        P(None, "grp"),
        P(None, ("grp", "ka")),
        P(("grp", "ka"), None, None),
        P(("grp", "ka")),
        P(("grp", "ka")),
    )
    return jax.shard_map(
        part,
        mesh=mesh,
        in_specs=placed,
        out_specs=P(("grp", "ka"), None, None, None),
        check_vma=False,
    )
```

profile of v0, /device:TPU:1, one launch (start us, length us, event | category | flops | bytes accessed | tf_op | source)
XLA Modules:
  0.0 209.7 jit_solution(6560134663480451760)
XLA Ops:
  0.0 0.9 convert_reduce_fusion
  0.9 0.7 multiply_add_fusion.flat_index
  1.6 0.0 copy-start
  1.6 0.8 select_reduce_fusion
  2.3 0.7 pad.9
  3.0 0.1 reshape.8
  3.1 0.7 pad_add_fusion.letters
  3.8 0.0 copy-done
  3.8 201.1 %shard_map.64 = f32[64,2,64,128]{3,2,1,0:T(8,128)} custom-call(f32[2,1024,512]{2,1,0:T(8,128)} %table_hbm.1, f32[64,64,128]{2,1,0:T(8,128)} %eigen_hbm.1, s32[16,8,128]{2,1,0:T(8,128)} %pad_add_fusion.letters, s32[3,1024]{1,0:T(4,128)} %lattice.1, s32[64]{0:T(128)} %copy-done), custom_call_target="tpu_custom_call" | custom-call | tf_op jit(solution)/shard_map/pallas_call | solution.py:452
  204.9 4.8 %copy.11 = f32[64,2,64,128]{3,2,1,0:T(8,128)} copy(f32[64,2,64,128]{3,2,1,0:T(8,128)} %shard_map.64) | data formatting | bytes 8388608
Async XLA Ops:
  1.6 2.2 %copy-start = (s32[64]{0:T(128)}, s32[64]{0:T(128)S(1)}, u32[]{:S(2)}) copy-start(s32[64]{0:T(128)S(1)} %multiply_add_fusion.flat_index) | copy-start | bytes 772
where the time goes:
time: 210 us
  Pallas kernels  201 us (96%)
  local copies, waits for them, and re-layouts  5.56 us (3%)
  other arithmetic  2.98 us (1%)
    pallas_call x1, Pallas kernels, fused(): pl.pallas_call(functools.partial(kernel, sizes), out_shape=jax.ShapeDtype...  201 us
    unnamed x3, local copies, waits for them, and re-layouts  4.79 us

commit v1 on v0

--- a/solution.py
+++ b/solution.py
@@ -138,14 +138,16 @@
     sizes,
     table_hbm,
     eigen_hbm,
-    letters,
+    grid_own,
     lattice,
-    flat_index,
+    owner_row,
+    slot_row,
     out_hbm,
     table,
     eigen,
     table_high,
     table_low,
+    letter,
     inbox,
     inbox_scalar,
     far_out,
@@ -170,7 +172,7 @@
     rows = pairs // orbitals
     wide = 2 * orbitals
     modes = n * rows // orbitals
-    per_chunk = kpoints // chunks
+    starts = [sum(chunks[:at]) for at in range(len(chunks))]
     me = lax.axis_index("ka")
 
     load_table = pltpu.make_async_copy(table_hbm, table, load_sem.at[0])
@@ -178,6 +180,28 @@
     load_eigen.start()
     load_table.start()
 
+    square = (128, 128)
+    owners = jnp.broadcast_to(
+        jnp.concatenate([owner_row[...], jnp.full((1, 128 - kpoints), n, jnp.int32)], 1), square
+    )
+    slots = jnp.broadcast_to(
+        jnp.concatenate([slot_row[...], jnp.zeros((1, 128 - kpoints), jnp.int32)], 1), square
+    )
+    owners_down, slots_down = owners.T, slots.T
+    lane = lax.broadcasted_iota(jnp.int32, square, 1)
+    down = lax.broadcasted_iota(jnp.int32, square, 0)
+    same = owners == owners_down
+    before = jnp.sum(jnp.where(same & (down < lane), 1, 0), 0, keepdims=True)
+    before_down = jnp.sum(jnp.where(same & (lane < down), 1, 0), 1, keepdims=True)
+    flat_row = owners[:1] * capacity + before
+    flat_down = owners_down * capacity + before_down
+    hit = (flat_down == lane) & (down < kpoints)
+    wanted = jnp.sum(jnp.where(hit, slots_down, 0), 0, keepdims=True)
+    letter[...] = jnp.zeros((8, 128), jnp.int32)
+    letter[0:3, 0:kpoints] = grid_own[...]
+    letter[3:4, :] = wanted
+    letter[4:5, :] = flat_row
+
     barrier = pltpu.get_barrier_semaphore()
 
     @pl.loop(1, n)
@@ -190,7 +214,7 @@
     def send_letter(step):
         other = lax.rem(me + step, n)
         return pltpu.make_async_remote_copy(
-            src_ref=letters.at[other],
+            src_ref=letter,
             dst_ref=inbox.at[me],
             send_sem=letter_send.at[other],
             recv_sem=letter_recv.at[me],
@@ -201,7 +225,7 @@
     def recv_letter(step):
         other = lax.rem(me + step, n)
         return pltpu.make_async_remote_copy(
-            src_ref=letters.at[other],
+            src_ref=letter,
             dst_ref=inbox.at[other],
             send_sem=letter_send.at[other],
             recv_sem=letter_recv.at[other],
@@ -233,7 +257,7 @@
 
     def entries(step, chunk, receive):
         other = lax.rem(me + step, n)
-        part = pl.ds(chunk * per_chunk * rows, per_chunk * rows)
+        part = pl.ds(starts[chunk] * rows, chunks[chunk] * rows)
         slot = other if receive else me
         return pltpu.make_async_remote_copy(
             src_ref=entries_out.at[other, part],
@@ -248,7 +272,7 @@
     def _(step):
         send_letter(step).start()
 
-    inbox[me] = letters[me]
+    inbox[me] = letter[...]
 
     @pl.loop(1, n)
     def _(step):
@@ -259,19 +283,15 @@
     to_scalar.wait()
     load_eigen.wait()
 
-    def far_order(step):
-        return lax.rem(step + n // 2, n)
-
     @pl.loop(0, n)
     def _(step):
-        offset = far_order(step)
-        other = lax.rem(me + offset, n)
+        other = lax.rem(me + step, n)
         for slot in range(capacity):
-            far_out[other, slot] = eigen[inbox_scalar[other, 3, slot]]
-
-        @pl.when(offset != 0)
+            far_out[other, slot] = eigen[inbox_scalar[other, 3, me * capacity + slot]]
+
+        @pl.when(step != 0)
         def _():
-            send_far(offset).start()
+            send_far(step).start()
 
     own_far = pltpu.make_async_copy(far_out.at[me], far_in.at[me], scalar_sem.at[1])
     own_far.start()
@@ -294,7 +314,7 @@
     @pl.loop(0, n // per_group)
     def _(group):
         for local_at in range(per_group):
-            other = lax.rem(me + far_order(group * per_group + local_at), n)
+            other = lax.rem(me + group * per_group + local_at, n)
             turned = inbox[other].T
             coords = [turned[:kpoints, axis : axis + 1] for axis in range(3)]
 
@@ -335,20 +355,16 @@
                 odd = jnp.where(first_half, pltpu.roll(real_part, orbitals, 1), imag_part)
                 row = first // orbitals + 2 * pair
                 for local_at in range(per_group):
-                    other = lax.rem(me + far_order(group * per_group + local_at), n)
+                    other = lax.rem(me + group * per_group + local_at, n)
                     own = slice(local_at * kpoints, (local_at + 1) * kpoints)
                     entries_out[other, pl.ds(row, kpoints, stride=rows), :] = even[own]
                     entries_out[other, pl.ds(row + 1, kpoints, stride=rows), :] = odd[own]
 
-    for chunk in range(chunks):
-
-        @pl.loop(0, n)
+    for chunk in range(len(chunks)):
+
+        @pl.loop(1, n)
         def _(step):
-            offset = far_order(step)
-
-            @pl.when(offset != 0)
-            def _():
-                entries(offset, chunk, False).start()
+            entries(step, chunk, False).start()
 
     own_entries = pltpu.make_async_copy(entries_out.at[me], entries_in.at[me], scalar_sem.at[2])
     own_entries.start()
@@ -371,7 +387,7 @@
 
     @pl.loop(0, kpoints)
     def _(k):
-        at = flat_index[k]
+        at = inbox_scalar[me, 4, k]
         far = far_in[at // capacity, lax.rem(at, capacity)]
         high = far.astype(jnp.bfloat16).astype(jnp.float32)
         far_parts[k] = jnp.concatenate([high, far - high], 0).T.astype(jnp.bfloat16)
@@ -396,24 +412,24 @@
             result[k, mode] = span[:orbitals] + jnp.where(half_lane, turned, -turned)
 
     def store(chunk):
-        part = pl.ds(chunk * per_chunk, per_chunk)
+        part = pl.ds(starts[chunk], chunks[chunk])
         return pltpu.make_async_copy(result.at[part], out_hbm.at[part], store_sem.at[chunk])
 
-    together = 2 if per_chunk % 2 == 0 else 1
-    for chunk in range(chunks):
+    for chunk in range(len(chunks)):
+        together = 2 if chunks[chunk] % 2 == 0 else 1
 
         @pl.loop(1, n)
         def _(step):
             entries(step, chunk, True).wait_recv()
 
-        @pl.loop(0, per_chunk // together)
+        @pl.loop(0, chunks[chunk] // together)
         def _(step):
             for extra in range(together):
-                rotate_one(chunk * per_chunk + step * together + extra)
+                rotate_one(starts[chunk] + step * together + extra)
 
         store(chunk).start()
 
-    for chunk in range(chunks):
+    for chunk in range(len(chunks)):
         store(chunk).wait()
 
         @pl.loop(1, n)
@@ -434,18 +450,8 @@
     rows = pairs // orbitals
     modes = n * rows // orbitals
     per_group = math.gcd(n, 4)
-    chunks = math.gcd(kpoints, 4)
-
-    ids = jnp.arange(kpoints, dtype=jnp.int32)
-    same = (target_owner[:, None] == target_owner[None, :]) & (ids[None, :] < ids[:, None])
-    position = jnp.sum(same.astype(jnp.int32), 1)
-    flat_index = target_owner * capacity + position
-    places = jnp.arange(n * capacity, dtype=jnp.int32)
-    wanted = jnp.sum(
-        jnp.where(places[:, None] == flat_index[None, :], target_slot[None, :], 0), 1
-    ).reshape(n, 1, capacity)
-    wanted = jnp.pad(wanted, ((0, 0), (3, 4), (0, 128 - capacity)))
-    letters = wanted + jnp.pad(kpoint_grid, ((0, 5), (0, 128 - kpoints)))[None]
+    last = max(kpoints // 16, 1)
+    chunks = [size for size in (kpoints - 10 * last, 6 * last, 3 * last, last) if size > 0]
 
     f32, bf16 = jnp.float32, jnp.bfloat16
     sizes = (n, kpoints, orbitals, vectors, pairs, capacity, per_group, chunks)
@@ -457,7 +463,8 @@
             pl.BlockSpec(memory_space=pl.ANY),
             pl.BlockSpec(memory_space=pltpu.VMEM),
             pl.BlockSpec(memory_space=pltpu.VMEM),
-            pl.BlockSpec(memory_space=pltpu.SMEM),
+            pl.BlockSpec(memory_space=pltpu.VMEM),
+            pl.BlockSpec(memory_space=pltpu.VMEM),
         ],
         out_specs=pl.BlockSpec(memory_space=pl.ANY),
         scratch_shapes=[
@@ -465,6 +472,7 @@
             pltpu.VMEM((kpoints, orbitals, wide), f32),
             pltpu.VMEM((2, vectors, pairs), bf16),
             pltpu.VMEM((2, vectors, pairs), bf16),
+            pltpu.VMEM((8, 128), jnp.int32),
             pltpu.VMEM((n, 8, 128), jnp.int32),
             pltpu.SMEM((n, 8, 128), jnp.int32),
             pltpu.VMEM((n, capacity, orbitals, wide), f32),
@@ -481,19 +489,31 @@
             pltpu.SemaphoreType.DMA((n,)),
             pltpu.SemaphoreType.DMA((n,)),
             pltpu.SemaphoreType.DMA((n,)),
-            pltpu.SemaphoreType.DMA((n, chunks)),
-            pltpu.SemaphoreType.DMA((n, chunks)),
-            pltpu.SemaphoreType.DMA((chunks,)),
+            pltpu.SemaphoreType.DMA((n, len(chunks))),
+            pltpu.SemaphoreType.DMA((n, len(chunks))),
+            pltpu.SemaphoreType.DMA((len(chunks),)),
         ],
         compiler_params=pltpu.CompilerParams(
             collective_id=0, has_side_effects=True, vmem_limit_bytes=60 * 1024 * 1024
         ),
-    )(wannier_table, eigen_vectors, letters, lattice, flat_index)
+    )(
+        wannier_table,
+        eigen_vectors,
+        kpoint_grid,
+        lattice,
+        target_owner.reshape(1, kpoints),
+        target_slot.reshape(1, kpoints),
+    )
 
 
 def part(wannier_table, lattice, kpoint_grid, eigen_vectors, target_owner, target_slot):
     rows = wannier_table.shape[2] // eigen_vectors.shape[1]
-    tiled = rows % 8 == 0 and wannier_table.shape[1] % 128 == 0 and eigen_vectors.shape[2] == 128
+    tiled = (
+        rows % 8 == 0
+        and wannier_table.shape[1] % 128 == 0
+        and eigen_vectors.shape[2] == 128
+        and 2 * eigen_vectors.shape[0] <= 128
+    )
     step = fused if tiled else local
     return step(wannier_table, lattice, kpoint_grid, eigen_vectors, target_owner, target_slot)
 

time: 210 us -> 202 us (0.962)
  Pallas kernels: 201 us -> 197 us
  other arithmetic: 2.98 us -> 0 us
    pallas_call x1, Pallas kernels: 201 us -> 197 us  [fused(): pl.pallas_call(functools.partial(kernel, sizes), out_shape=jax.ShapeDtype...]
    unnamed x3 -> x1, local copies, waits for them, and re-layouts: 4.79 us -> 4.79 us
where the time goes in v1:
time: 202 us
  Pallas kernels  197 us (98%)
  local copies, waits for them, and re-layouts  4.79 us (2%)
    pallas_call x1, Pallas kernels, fused(): pl.pallas_call(functools.partial(kernel, sizes), out_shape=jax.ShapeDtype...  197 us
    unnamed x1, local copies, waits for them, and re-layouts  4.79 us

profile of v1, /device:TPU:1, one launch (start us, length us, event | category | flops | bytes accessed | tf_op | source)
XLA Modules:
  0.0 201.6 jit_solution(12371034747911264028)
XLA Ops:
  0.0 196.8 %shard_map.64 = f32[64,2,64,128]{3,2,1,0:T(8,128)} custom-call(f32[2,1024,512]{2,1,0:T(8,128)} %table_hbm.1, f32[64,64,128]{2,1,0:T(8,128)} %eigen_hbm.1, s32[3,64]{1,0:T(4,128)} %grid_own.1, s32[3,1024]{1,0:T(4,128)} %lattice.1, s32[1,64]{1,0:T(1,128)} %bitcast.2, s32[1,64]{1,0:T(1,128)} %bitcast.3), custom_call_target="tpu_custom_call" | custom-call | tf_op jit(solution)/shard_map/pallas_call | solution.py:458
  196.8 4.8 %copy.8 = f32[64,2,64,128]{3,2,1,0:T(8,128)} copy(f32[64,2,64,128]{3,2,1,0:T(8,128)} %shard_map.64) | data formatting | bytes 8388608
